TPU v7x, 128 devices: a whole 4x4x4 slice. The times are simulated.
128 devices in a mesh: row: 32 (over x_hi, y, z), col: 4 (over x_lo, core).
Axes of the slice: x: 4 (x_hi: 2, x_lo: 2; x = x_hi * 2 + x_lo), y: 4, z: 4, core: 2. Of those that a mesh axis runs over, the one named last changes fastest.
Arguments:
- atom_feats: bfloat16 [20480, 128], P('row'), may hold values from -6 to 6
- atom_gain: float32 [128], replicated, may hold values from 0.1 to 1.9
- w_atom: bfloat16 [3, 128, 128], P(None, None, 'col'), may hold values from -0.5 to 0.5
- atom_pair: bfloat16 [16, 20480, 128], P(None, 'row'), may hold values from -80 to 80
- w_atom_bias: bfloat16 [16, 4], P(None, 'col'), may hold values from -2 to 2
- atom_counts: int32 [2560], P('row'), may hold values from 2 to 24, as said below
- token_single: bfloat16 [2560, 768], P('row'), may hold values from -3 to 3
- w_pool: bfloat16 [128, 768], replicated, may hold values from -2 to 2
- token_gain: float32 [2, 768], replicated, may hold values from 0.1 to 1.9
- w_attn: bfloat16 [2, 4, 768, 768], P(None, None, None, 'col'), may hold values from -0.21875 to 0.21875
- w_out: bfloat16 [2, 768, 768], P(None, 'col'), may hold values from -0.21875 to 0.21875
- pair: bfloat16 [2560, 2560, 128], P('row', 'col'), may hold values from -30 to 30
- w_bias: bfloat16 [2, 128, 16], replicated, may hold values from -1 to 1
Outputs:
- tokens_out: bfloat16 [2560, 768], P('row')
Inputs may be any that keep to these rules, and one draw needn't show every extreme that they name: `atom_counts`: the first 640 tokens have 24 atoms each, every other token 2 or 3; counts sum to 20480.
All inputs are finite; a program needn't handle non-finite values.
Results may differ from a plain program's by a relative error of at most 0.02.
Values may be sent and summed in bfloat16 or wider, within the bound.
No kernel may reach another device: no remote copies, remote signals or barrier semaphores. Data moves between devices by JAX's collectives and lax.ppermute only.
A program may use at most 128 MiB of HBM per device.

v0:
```python
import math

import jax
import jax.numpy as jnp
from jax import lax
from jax.sharding import PartitionSpec as P

QBLOCK = 32
WK = 128
REACH = 48


epsilon = 1e-05


def extended(cells, sides, width):
    for axis, dim in sides:
        count = lax.axis_size(axis)
        ends = count - 1
        head = lax.slice_in_dim(cells, 0, width, axis=dim)
        tail = lax.slice_in_dim(cells, cells.shape[dim] - width, cells.shape[dim], axis=dim)
        cells = jnp.concatenate(
            [
                lax.ppermute(tail, axis, [(i, (i + 1) % count) for i in range(ends)]),
                cells,
                lax.ppermute(head, axis, [((i + 1) % count, i) for i in range(ends)]),
            ],
            axis=dim,
        )
    return cells


def layer_norm(values, gain_row):
    values = values.astype(jnp.float32)
    centred = values - jnp.mean(values, axis=-1, keepdims=True)
    spread = jnp.mean(centred * centred, axis=-1, keepdims=True)
    return centred * lax.rsqrt(spread + epsilon) * gain_row


def softmax_rows(scores):
    row_max = jnp.max(scores, axis=-1, keepdims=True)
    weights = jnp.exp(scores - row_max)
    return (weights / jnp.sum(weights, axis=-1, keepdims=True)).astype(jnp.bfloat16)


def on_device(
    atom_feats,
    atom_gain,
    w_atom,
    atom_pair,
    w_atom_bias,
    atom_counts,
    token_single,
    w_pool,
    token_gain,
    w_attn,
    w_out,
    pair,
    w_bias,
):
    atom_rows = atom_feats.shape[0]
    head_cols = w_atom.shape[2]
    atom_heads = w_atom_bias.shape[1]
    atom_head_size = head_cols // atom_heads
    layer_total = w_bias.shape[0]
    normed_atoms = layer_norm(atom_feats, atom_gain).astype(jnp.bfloat16)
    atom_q = jnp.dot(normed_atoms, w_atom[0], preferred_element_type=jnp.float32).astype(
        jnp.bfloat16
    )
    atom_k = jnp.dot(normed_atoms, w_atom[1], preferred_element_type=jnp.float32).astype(
        jnp.bfloat16
    )
    atom_v = jnp.dot(normed_atoms, w_atom[2], preferred_element_type=jnp.float32).astype(
        jnp.bfloat16
    )
    joined = jnp.concatenate([atom_k, atom_v], axis=1)
    padded = extended(joined, (("row", 0),), REACH)
    blocks = atom_rows // QBLOCK
    atom_tiles = padded.reshape(blocks + WK // QBLOCK - 1, QBLOCK, 2 * head_cols)
    windows = jnp.concatenate(
        [atom_tiles[offset : offset + blocks] for offset in range(WK // QBLOCK)], axis=1
    )
    key_win = windows[:, :, :head_cols].reshape(blocks, WK, atom_heads, atom_head_size)
    value_win = windows[:, :, head_cols:].reshape(blocks, WK, atom_heads, atom_head_size)
    query_blk = atom_q.reshape(blocks, QBLOCK, atom_heads, atom_head_size)
    atom_bias = jnp.einsum(
        "cak,ch->hak", atom_pair, w_atom_bias, preferred_element_type=jnp.float32
    )
    atom_bias = jnp.transpose(atom_bias.reshape(atom_heads, blocks, QBLOCK, WK), (1, 0, 2, 3))
    first_atom = lax.axis_index("row") * atom_rows
    total_atoms = atom_rows * lax.axis_size("row")
    keys_at = (
        first_atom
        + QBLOCK * jnp.arange(blocks, dtype=jnp.int32)[:, None]
        - REACH
        + jnp.arange(WK, dtype=jnp.int32)[None, :]
    )
    in_range = (keys_at >= 0) & (keys_at < total_atoms)
    atom_scores = (
        jnp.einsum("bqhd,bkhd->bhqk", query_blk, key_win, preferred_element_type=jnp.float32)
        / math.sqrt(atom_head_size)
        + atom_bias
    )
    atom_scores = jnp.where(in_range[:, None, None, :], atom_scores, -1e30)
    atom_probs = softmax_rows(atom_scores)
    atom_out = jnp.einsum(
        "bhqk,bkhd->bqhd", atom_probs, value_win, preferred_element_type=jnp.float32
    )
    atom_out = atom_out.reshape(atom_rows, head_cols).astype(jnp.bfloat16)
    all_counts = lax.all_gather(atom_counts, "row", axis=0, tiled=True)
    seg_ends = jnp.cumsum(all_counts)
    seg_starts = seg_ends - all_counts
    atom_index = first_atom + jnp.arange(atom_rows, dtype=jnp.int32)
    member = (
        (atom_index[None, :] >= seg_starts[:, None]) & (atom_index[None, :] < seg_ends[:, None])
    ).astype(jnp.bfloat16)
    token_sums = lax.psum_scatter(
        jnp.dot(member, atom_out, preferred_element_type=jnp.float32).astype(jnp.bfloat16),
        "row",
        scatter_dimension=0,
        tiled=True,
    ).astype(jnp.float32)
    pooled = (token_sums / atom_counts.astype(jnp.float32)[:, None]).astype(jnp.bfloat16)
    pool_rows = lax.dynamic_slice_in_dim(w_pool, lax.axis_index("col") * head_cols, head_cols, 0)
    projected_pool = lax.psum(
        jnp.dot(pooled, pool_rows, preferred_element_type=jnp.float32).astype(jnp.bfloat16), "col"
    ).astype(jnp.float32)
    residual = token_single.astype(jnp.float32) + projected_pool
    tok_rows = residual.shape[0]
    head_total = w_bias.shape[2]
    head_count = head_total // lax.axis_size("col")
    tok_head = w_attn.shape[3] // head_count
    for layer_idx in range(layer_total):
        normed = layer_norm(residual, token_gain[layer_idx]).astype(jnp.bfloat16)
        projected = jnp.einsum(
            "tc,fcd->ftd", normed, w_attn[layer_idx], preferred_element_type=jnp.float32
        ).astype(jnp.bfloat16)
        keys_all, values_all = (
            lax.all_gather(projected[1], "row", axis=0, tiled=True),
            lax.all_gather(projected[2], "row", axis=0, tiled=True),
        )
        local_bias = jnp.einsum(
            "ijc,ch->hij", pair, w_bias[layer_idx], preferred_element_type=jnp.float32
        ).astype(jnp.bfloat16)
        pair_bias = lax.all_to_all(local_bias, "col", split_axis=0, concat_axis=2, tiled=True)
        queries = projected[0].reshape(tok_rows, head_count, tok_head)
        key_heads = keys_all.reshape(-1, head_count, tok_head)
        value_heads = values_all.reshape(-1, head_count, tok_head)
        scores = jnp.einsum(
            "thd,nhd->htn", queries, key_heads, preferred_element_type=jnp.float32
        ) / math.sqrt(tok_head) + pair_bias.astype(jnp.float32)
        token_probs = softmax_rows(scores)
        mixture = jnp.einsum(
            "htn,nhd->thd", token_probs, value_heads, preferred_element_type=jnp.float32
        ).reshape(tok_rows, head_count * tok_head)
        gated = (mixture * jax.nn.sigmoid(projected[3].astype(jnp.float32))).astype(jnp.bfloat16)
        partial_out = jnp.dot(gated, w_out[layer_idx], preferred_element_type=jnp.float32)
        residual = residual + lax.psum(partial_out.astype(jnp.bfloat16), "col").astype(jnp.float32)
    return residual.astype(jnp.bfloat16)


def solution(mesh):
    placed = (
        P("row", None),
        P(),
        P(None, None, "col"),
        P(None, "row", None),
        P(None, "col"),
        P("row"),
        P("row", None),
        P(),
        P(),
        P(None, None, None, "col"),
        P(None, "col", None),
        P("row", "col", None),
        P(),
    )
    return jax.shard_map(
        on_device, mesh=mesh, in_specs=placed, out_specs=P("row", None), check_vma=False
    )
```

profile of v0, /device:TPU:1, one launch (start us, length us, event | category | flops | bytes accessed | tf_op | source)
XLA Modules:
  0.0 984.0 jit_solution(18257932389388564335)
XLA Ops:
  12.0 4.4 collective-permute-start
  21.4 157.5 %all-reduce = s32[2560]{0:T(1024)S(1)} all-reduce(s32[2560]{0:T(1024)S(1)} %dynamic-update-slice), channel_id=1, replica_groups=mesh['row'=32,'col'=4] {'row'}, use_global_device_ids=true, to_apply=%add | all-reduce | flops 2560 | bytes 20480
  199.3 2.9 fusion.10
  203.3 8.2 convolution_convert_fusion.1
  213.1 33.5 %all-to-all-start = ((bf16[16,80,640]{2,1,0:T(8,128)(2,1)}), bf16[16,80,640]{2,1,0:T(8,128)(2,1)}, u32[]{:S(2)}, u32[]{:S(2)}) async-start(bf16[16,80,640]{2,1,0:T(8,128)(2,1)} %copy.84), calls=%async_computation | async-start | bytes 3276800 | tf_op jit(solution)/shard_map/all_to_all | solution.py:145
  246.7 140.5 %reduce-scatter.4.cloned.1.call-done = bf16[80,32]{1,0:T(8,128)(2,1)} async-done(((bf16[2560,32]{1,0:T(8,128)(2,1)}), bf16[80,32]{1,0:T(8,128)(2,1)}) %reduce-scatter.4.cloned.1.call-update) | async-done | bytes 5136
  389.6 8.2 convolution_convert_fusion
  399.4 45.5 %all-reduce.5.cloned.1.call-done = bf16[80,768]{1,0:T(8,128)(2,1)} async-done(((bf16[80,768]{1,0:T(8,128)(2,1)}), bf16[80,768]{1,0:T(8,128)(2,1)}) %all-reduce.5.cloned.1.call-update) | async-done | bytes 122896 | tf_op jit(solution)/shard_map/psum | solution.py:125
  449.1 93.5 %all-gather = bf16[1,2560,192]{2,1,0:T(8,128)(2,1)} all-gather(bf16[1,80,192]{2,1,0:T(8,128)(2,1)S(1)} %get-tuple-element.14), channel_id=2, replica_groups=mesh['row'=32,'col'=4] {'row'}, dimensions={1}, use_global_device_ids=true | all-gather | bytes 1013760 | tf_op jit(solution)/shard_map/all_gather | solution.py:140
  545.1 86.0 %all-gather.1 = bf16[1,2560,192]{2,1,0:T(8,128)(2,1)} all-gather(bf16[1,80,192]{2,1,0:T(8,128)(2,1)S(1)} %get-tuple-element.12), channel_id=3, replica_groups=mesh['row'=32,'col'=4] {'row'}, dimensions={1}, use_global_device_ids=true | all-gather | bytes 1013760 | tf_op jit(solution)/shard_map/all_gather | solution.py:139
  631.1 2.4 copy.83
  633.5 31.5 %all-to-all-start.1 = ((bf16[16,80,640]{2,1,0:T(8,128)(2,1)}), bf16[16,80,640]{2,1,0:T(8,128)(2,1)}, u32[]{:S(2)}, u32[]{:S(2)}) async-start(bf16[16,80,640]{2,1,0:T(8,128)(2,1)} %copy.90), calls=%async_computation.1 | async-start | bytes 3276800 | tf_op jit(solution)/shard_map/all_to_all | solution.py:145
  665.0 4.4 copy.104
  669.4 5.2 reshape.195
  674.5 2.9 fusion.7
  679.8 4.2 fusion.46
  685.0 4.4 copy.103
  689.4 5.2 reshape.198
  694.6 22.8 %all-reduce.7.cloned.1.call-done = bf16[80,768]{1,0:T(8,128)(2,1)} async-done(((bf16[80,768]{1,0:T(8,128)(2,1)}), bf16[80,768]{1,0:T(8,128)(2,1)}) %all-reduce.7.cloned.1.call-update) | async-done | bytes 122896 | tf_op jit(solution)/shard_map/psum | solution.py:158
  721.7 93.5 %all-gather.2 = bf16[1,2560,192]{2,1,0:T(8,128)(2,1)} all-gather(bf16[1,80,192]{2,1,0:T(8,128)(2,1)S(1)} %get-tuple-element.11), channel_id=4, replica_groups=mesh['row'=32,'col'=4] {'row'}, dimensions={1}, use_global_device_ids=true | all-gather | bytes 1013760 | tf_op jit(solution)/shard_map/all_gather | solution.py:140
  817.7 86.2 %all-gather.3 = bf16[1,2560,192]{2,1,0:T(8,128)(2,1)} all-gather(bf16[1,80,192]{2,1,0:T(8,128)(2,1)S(1)} %get-tuple-element.9), channel_id=5, replica_groups=mesh['row'=32,'col'=4] {'row'}, dimensions={1}, use_global_device_ids=true | all-gather | bytes 1013760 | tf_op jit(solution)/shard_map/all_gather | solution.py:139
  906.3 2.9 fusion.6
  911.5 4.2 fusion.45
  917.5 58.3 %all-reduce.9.cloned.1.call-done = bf16[80,768]{1,0:T(8,128)(2,1)} async-done(((bf16[80,768]{1,0:T(8,128)(2,1)}), bf16[80,768]{1,0:T(8,128)(2,1)}) %all-reduce.9.cloned.1.call-update) | async-done | bytes 122896 | tf_op jit(solution)/shard_map/psum | solution.py:158
  (106 shorter events, 61.5 us)
Async XLA Ops:
  6.5 173.0 %copy-start = (bf16[16,640,128]{2,1,0:T(8,128)(2,1)S(1)}, bf16[16,640,128]{2,1,0:T(8,128)(2,1)}, u32[]{:S(2)}) copy-start(bf16[16,640,128]{2,1,0:T(8,128)(2,1)} %param.16) | copy-start | bytes 7864324
  6.5 380.6 %reduce-scatter.4.cloned.1.call-start = ((), (), s32[]{:S(2)}) async-start(), calls=%async_computation.6 | async-start | bytes 675840
  12.0 170.0 %collective-permute-start = (bf16[48,64]{0,1:T(8,128)(2,1)S(1)}, bf16[48,64]{0,1:T(8,128)(2,1)S(1)}, u32[]{:S(2)}, u32[]{:S(2)}) collective-permute-start(bf16[48,64]{0,1:T(8,128)(2,1)S(1)} %get-tuple-element.21), channel_id=1, source_target_pairs={{0,4},{4,8},{8,12},{12,16},{16,20},{20,24},{24,28},{28,32},{32,36}... | collective-permute-start | bytes 18440 | tf_op jit(solution)/shard_map/ppermute | solution.py:24
  16.3 165.6 %collective-permute-start.1 = (bf16[48,64]{0,1:T(8,128)(2,1)S(1)}, bf16[48,64]{0,1:T(8,128)(2,1)S(1)}, u32[]{:S(2)}, u32[]{:S(2)}) collective-permute-start(bf16[48,64]{0,1:T(8,128)(2,1)S(1)} %get-tuple-element.22), channel_id=1, source_target_pairs={{4,0},{8,4},{12,8},{16,12},{20,16},{24,20},{28,24},{32,28},{36,32}... | collective-permute-start | bytes 18440 | tf_op jit(solution)/shard_map/ppermute | solution.py:26
  196.0 0.7 copy-start.6
  199.3 4.1 copy-start.8
  211.6 35.1 %copy-start.10 = (s32[80]{0:T(128)S(1)}, s32[80]{0:T(128)}, u32[]{:S(2)}) copy-start(s32[80]{0:T(128)} %param.18) | copy-start | bytes 964
  213.1 420.4 %all-to-all-start = ((bf16[16,80,640]{2,1,0:T(8,128)(2,1)}), bf16[16,80,640]{2,1,0:T(8,128)(2,1)}, u32[]{:S(2)}, u32[]{:S(2)}) async-start(bf16[16,80,640]{2,1,0:T(8,128)(2,1)} %copy.84), calls=%async_computation | async-start | bytes 3276800 | tf_op jit(solution)/shard_map/all_to_all | solution.py:145
  246.6 198.3 %all-reduce.5.cloned.1.call-start = ((), (), s32[]{:S(2)}) async-start(), calls=%async_computation.3 | async-start | bytes 245760 | tf_op jit(solution)/shard_map/psum | solution.py:125
  397.8 1.5 copy-start.9
  397.9 47.1 %copy-start.3 = (bf16[80,768]{1,0:T(8,128)(2,1)S(1)}, bf16[80,768]{1,0:T(8,128)(2,1)}, u32[]{:S(2)}) copy-start(bf16[80,768]{1,0:T(8,128)(2,1)} %param.19) | copy-start | bytes 368644
  633.5 51.5 %all-to-all-start.1 = ((bf16[16,80,640]{2,1,0:T(8,128)(2,1)}), bf16[16,80,640]{2,1,0:T(8,128)(2,1)}, u32[]{:S(2)}, u32[]{:S(2)}) async-start(bf16[16,80,640]{2,1,0:T(8,128)(2,1)} %copy.90), calls=%async_computation.1 | async-start | bytes 3276800 | tf_op jit(solution)/shard_map/all_to_all | solution.py:145
  665.0 52.4 %all-reduce.7.cloned.1.call-start = ((), (), s32[]{:S(2)}) async-start(), calls=%async_computation.4 | async-start | bytes 245760 | tf_op jit(solution)/shard_map/psum | solution.py:158
  677.4 1.7 copy-start.1
  679.7 4.2 copy-start.7
  684.9 291.0 %all-reduce.9.cloned.1.call-start = ((), (), s32[]{:S(2)}) async-start(), calls=%async_computation.5 | async-start | bytes 245760 | tf_op jit(solution)/shard_map/psum | solution.py:158
  689.4 28.0 %copy-start.4 = (bf16[80,768]{1,0:T(8,128)(2,1)S(1)}, bf16[80,768]{1,0:T(8,128)(2,1)}, u32[]{:S(2)}) copy-start(bf16[80,768]{1,0:T(8,128)(2,1)} %all-reduce.5.cloned.1.call-done) | copy-start | bytes 368644
  909.1 1.7 copy-start.2
  911.5 64.4 %copy-start.5 = (bf16[80,768]{1,0:T(8,128)(2,1)S(1)}, bf16[80,768]{1,0:T(8,128)(2,1)}, u32[]{:S(2)}) copy-start(bf16[80,768]{1,0:T(8,128)(2,1)} %all-reduce.7.cloned.1.call-done) | copy-start | bytes 368644
Sparse Core Ops, SparseCore 0:
  203.4 183.6 reduce-scatter.3
  389.7 55.1 all-reduce.4
  685.0 32.3 all-reduce.6
  917.7 58.1 all-reduce.8
where the time goes:
time: 986 us; the launch traced here: 984 us
  blocking collectives  517 us (52%)
  waiting for transfers between devices  267 us (27%)
  starting transfers between devices  70.7 us (7%)
  local copies, waits for them, and re-layouts  52.9 us (5%)
  matrix products  48.8 us (5%)
  between operations  14.1 us (1%)
  other arithmetic  13.5 us (1%)
    all_gather x2, blocking collectives, on_device(): lax.all_gather(projected[2], 'row', axis=0, tiled=True)  187 us
    all_gather x2, blocking collectives, on_device(): lax.all_gather(projected[1], 'row', axis=0, tiled=True)  172 us
    unnamed x1, blocking collectives  158 us
    unnamed x5, waiting for transfers between devices  141 us
    psum x2, waiting for transfers between devices, on_device(): lax.psum(partial_out.astype(jnp.bfloat16), 'col').astype(jnp.float32)  81.1 us
    all_to_all x2, starting transfers between devices, on_device(): lax.all_to_all(local_bias, 'col', split_axis=0, concat_axis=2, tiled=True)  65 us
    psum x1, waiting for transfers between devices, on_device(): lax.psum(jnp.dot(pooled, pool_rows, preferred_element_type=jnp.float32).a...  45.5 us
  transfers between devices with their start and end apart: 8, of which 5 were waited for; matrix products, arithmetic and copies ran while one was open for 7% of the time, Pallas kernels for 0%

commit v1 on v0

v1 whole, which is shorter than its diff:
```python
import functools
import math

import jax
import jax.numpy as jnp
from jax import lax
from jax.experimental import pallas as pl
from jax.experimental.pallas import tpu as pltpu
from jax.sharding import Mesh
from jax.sharding import PartitionSpec as P

QBLOCK = 32
WK = 128
REACH = 48
EPSILON = 1e-05
NQ, NK, NC = 8, 4, 4
BF = jnp.bfloat16
F32 = jnp.float32
VMEM_LIMIT = 56 * 1024 * 1024
NT = (((1,), (1,)), ((), ()))
TN = (((0,), (0,)), ((), ()))


def dot(a, b, dims=(((1,), (0,)), ((), ()))):
    return lax.dot_general(a, b, dims, preferred_element_type=F32)


def layer_norm(values, gain_row):
    centred = values - jnp.mean(values, axis=-1, keepdims=True)
    spread = jnp.mean(centred * centred, axis=-1, keepdims=True)
    return centred * lax.rsqrt(spread + EPSILON) * gain_row


def call(kernel, out_shape, flops, moved, **kw):
    return pl.pallas_call(
        kernel,
        out_shape=out_shape,
        compiler_params=pltpu.CompilerParams(vmem_limit_bytes=VMEM_LIMIT),
        cost_estimate=pl.CostEstimate(flops=flops, bytes_accessed=moved, transcendentals=0),
        **kw,
    )


def shaped(shape, dtype):
    return jax.ShapeDtypeStruct(shape, dtype)


def pair_bias_kernel(pair_ref, w_ref, out_ref):
    rows = pair_ref.shape[0]
    w = w_ref[...]
    for i in range(rows):
        bias = dot(w, pair_ref[i], NT).astype(BF)
        out_ref[0, :, i, :] = bias[:16]
        out_ref[1, :, i, :] = bias[16:]


def pair_bias_call(pair, w_t):
    rows, cols, ch = pair.shape
    step = 16
    return pl.pallas_call(
        pair_bias_kernel,
        grid=(rows // step,),
        in_specs=[
            pl.BlockSpec((step, cols, ch), lambda i: (i, 0, 0)),
            pl.BlockSpec((32, ch), lambda i: (0, 0)),
        ],
        out_specs=pl.BlockSpec((2, 16, step, cols), lambda i: (0, 0, i, 0)),
        out_shape=shaped((2, 16, rows, cols), BF),
        compiler_params=pltpu.CompilerParams(vmem_limit_bytes=VMEM_LIMIT),
        cost_estimate=pl.CostEstimate(
            flops=2 * rows * cols * ch * 32, bytes_accessed=2 * rows * cols * (ch + 32), transcendentals=0
        ),
    )(pair, w_t)


def atom_kernel(first_ref, wab_ref, feats_ref, prev_ref, next_ref, gain_ref, w_ref, apair_ref, starts_ref, ends_ref, out_ref):
    rows = feats_ref.shape[0]
    first = first_ref[0]
    total = rows * NQ * NK
    x = jnp.concatenate([prev_ref[...], feats_ref[...], next_ref[...]], axis=0).astype(F32)
    normed = layer_norm(x, gain_ref[...]).astype(BF)
    q = dot(normed[REACH : REACH + rows], w_ref[0]).astype(BF)
    k = dot(normed, w_ref[1]).astype(BF)
    v = dot(normed, w_ref[2]).astype(BF)
    bias = apair_ref[0].astype(F32) * wab_ref[0]
    for c in range(1, apair_ref.shape[0]):
        bias += apair_ref[c].astype(F32) * wab_ref[c]
    scores = jnp.concatenate(
        [dot(q[at : at + QBLOCK], k[at : at + WK], NT) for at in range(0, rows, QBLOCK)], axis=0
    )
    scores = scores * (1.0 / math.sqrt(q.shape[1])) + bias
    at = lax.broadcasted_iota(jnp.int32, (rows, WK), 0) // QBLOCK * QBLOCK
    key_at = at + lax.broadcasted_iota(jnp.int32, (rows, WK), 1) + (first - REACH)
    scores = jnp.where((key_at >= 0) & (key_at < total), scores, -1e30)
    weights = jnp.exp(scores - jnp.max(scores, axis=-1, keepdims=True))
    probs = (weights / jnp.sum(weights, axis=-1, keepdims=True)).astype(BF)
    out = jnp.concatenate(
        [dot(probs[at : at + QBLOCK], v[at : at + WK]) for at in range(0, rows, QBLOCK)], axis=0
    )
    out_t = out.T.astype(BF)
    span = starts_ref.shape[2]
    index = lax.broadcasted_iota(jnp.int32, (rows, span), 0) + first
    for part in range(NQ):
        member = (index >= starts_ref[part]) & (index < ends_ref[part])
        member = jnp.where(member, 1.0, 0.0).astype(BF)
        out_ref[part] = dot(out_t, member).astype(BF)


def smem():
    return pl.BlockSpec(memory_space=pltpu.SMEM)


def vmem():
    return pl.BlockSpec(memory_space=pltpu.VMEM)


def project(residual, gain, w, kv_ref, qg_ref, width):
    normed = layer_norm(residual, gain).astype(BF)
    out = dot(normed, w).astype(BF)
    kv_ref[...] = out[:, : 2 * width]
    qg_ref[...] = out[:, 2 * width :]


def first_kernel(sums_ref, counts_ref, single_ref, w_pool_ref, gain_ref, w_ref, res_ref, kv_ref, qg_ref):
    sums = sums_ref[0].astype(F32)
    for k in range(1, NK):
        sums += sums_ref[k].astype(F32)
    pooled = (sums / counts_ref[...]).astype(BF)
    residual = single_ref[...].astype(F32) + dot(pooled, w_pool_ref[...], TN)
    res_ref[...] = residual
    project(residual, gain_ref[...], w_ref[...], kv_ref, qg_ref, kv_ref.shape[1] // 2)


def attend_kernel(qg_ref, kv_ref, bias_ref, out_ref):
    width = qg_ref.shape[1] // 2
    rows = bias_ref.shape[1]
    cols = bias_ref.shape[2]
    keys = kv_ref[:, :width]
    values = kv_ref[:, width:]
    for part in range(NK):
        q = qg_ref[part * rows : (part + 1) * rows, :width]
        scores = dot(q, keys, NT) * (1.0 / math.sqrt(width))
        bias = jnp.concatenate([bias_ref[part * NC + c] for c in range(NC)], axis=1)
        scores = scores + bias.astype(F32)
        weights = jnp.exp(scores - jnp.max(scores, axis=-1, keepdims=True))
        probs = (weights * (1.0 / jnp.sum(weights, axis=-1, keepdims=True))).astype(BF)
        mixture = dot(probs, values)
        gates = qg_ref[part * rows : (part + 1) * rows, width:].astype(F32)
        out_ref[part] = (mixture * jax.nn.sigmoid(gates)).T.astype(BF)


def middle_kernel(res_ref, gated_ref, w_out_ref, gain_ref, w_ref, out_ref, kv_ref, qg_ref):
    rows = gated_ref.shape[2]
    for part in range(NK):
        at = slice(part * rows, (part + 1) * rows)
        out_ref[at] = res_ref[at] + dot(gated_ref[part], w_out_ref[...], TN)
    project(out_ref[...], gain_ref[...], w_ref[...], kv_ref, qg_ref, kv_ref.shape[1] // 2)


def last_kernel(res_ref, gated_ref, w_out_ref, out_ref):
    out_ref[...] = (res_ref[...] + dot(gated_ref[...], w_out_ref[...], TN)).astype(BF)


def spread_all(x, axis, n):
    return lax.all_to_all(jnp.broadcast_to(x[None], (n,) + x.shape), axis, 0, 0, tiled=True)


def on_device(
    atom_feats, atom_gain, w_atom, atom_pair, w_atom_bias, atom_counts, token_single,
    w_pool, token_gain, w_attn, w_out, pair, w_bias,
):
    row_axes = ("q", "k")
    n_rows = NQ * NK
    q_at, k_at = lax.axis_index("q"), lax.axis_index("k")
    row_at = q_at * NK + k_at
    atom_rows, width_a = atom_feats.shape
    tq, ct = token_single.shape
    layers, ch, heads = w_bias.shape
    hd = ct // heads
    span = tq * NK

    prev = lax.ppermute(atom_feats[atom_rows - REACH :], row_axes, [(i, i + 1) for i in range(n_rows - 1)])
    nxt = lax.ppermute(atom_feats[:REACH], row_axes, [(i + 1, i) for i in range(n_rows - 1)])
    counts = jnp.pad(atom_counts, (0, 128 - tq))[None, None]
    counts = jnp.broadcast_to(counts, (n_rows, 8, 128))
    all_counts = lax.all_to_all(counts, row_axes, 0, 0, tiled=True)[:, 0, :tq].reshape(-1)
    singles = lax.all_gather(token_single, "k", axis=0, tiled=True)
    w_out_all = [
        lax.all_gather(w_out[l], "col", axis=0, tiled=False)
        .reshape(NC, NK, hd, ct).transpose(1, 0, 2, 3).reshape(ct, ct)
        for l in range(layers)
    ]
    w_own = lax.dynamic_slice_in_dim(w_attn, k_at * hd, hd, 3)
    w_cat = [
        jnp.concatenate([w_own[l, 1], w_own[l, 2], w_own[l, 0], w_own[l, 3]], axis=1) for l in range(layers)
    ]

    w_t = w_bias.reshape(layers, ch, NC, NK).transpose(0, 3, 2, 1).reshape(layers * heads, ch)
    local_bias = pair_bias_call(pair, w_t)
    bias = [lax.all_to_all(local_bias[l], ("k", "col"), 0, 0, tiled=True) for l in range(layers)]

    seg_ends = jnp.cumsum(all_counts)
    seg_starts = seg_ends - all_counts
    ends = seg_ends.reshape(NQ, 1, span)
    starts = seg_starts.reshape(NQ, 1, span)
    head_a = w_atom.shape[2]
    partial = call(
        atom_kernel,
        shaped((NQ, head_a, span), BF),
        2 * atom_rows * (3 * width_a * head_a + 2 * WK * head_a + head_a * NQ * span),
        2 * atom_pair.size,
        in_specs=[smem(), smem()] + [vmem()] * 8,
        out_specs=vmem(),
    )(
        (row_at * atom_rows).astype(jnp.int32)[None],
        w_atom_bias[:, 0].astype(F32),
        atom_feats, prev, nxt, atom_gain[None], w_atom, atom_pair, starts, ends,
    )
    sums = lax.all_to_all(partial, "q", 0, 0, tiled=True)
    sums = jnp.sum(sums.astype(F32), axis=0).astype(BF)
    sums = spread_all(sums, ("k", "col"), NK * NC).reshape(NK, width_a, span)
    own_counts = lax.dynamic_slice_in_dim(all_counts, q_at * span, span, 0).astype(F32)[None]

    proj_shapes = [shaped((span, ct), F32), shaped((span, 2 * hd), BF), shaped((span, 2 * hd), BF)]
    residual, kv, qg = call(first_kernel, proj_shapes, 2 * span * ct * 320, 2 * ct * 1000)(
        sums, own_counts, singles, w_pool, token_gain[0:1], w_cat[0]
    )
    for l in range(layers):
        kv = spread_all(kv, "q", NQ).reshape(NQ * span, 2 * hd)
        gated = call(
            attend_kernel, shaped((NK, hd, tq), BF), 4 * span * NQ * span * hd, 2 * bias[l].size
        )(qg, kv, bias[l])
        if l + 1 < layers:
            gated = spread_all(gated, ("k", "col"), NK * NC)
            gated = gated.transpose(1, 0, 2, 3).reshape(NK, ct, tq)
            residual, kv, qg = call(middle_kernel, proj_shapes, 2 * span * ct * 960, 2 * ct * 2000)(
                residual, gated, w_out_all[l], token_gain[l + 1 : l + 2], w_cat[l + 1]
            )
        else:
            gated = jnp.broadcast_to(gated[:, None], (NK, NC, hd, tq)).reshape(NK * NC, hd, tq)
            gated = lax.all_to_all(gated, ("k", "col"), 0, 0, tiled=True).reshape(ct, tq)
            own = lax.dynamic_slice_in_dim(residual, k_at * tq, tq, 0)
            return call(last_kernel, shaped((tq, ct), BF), 2 * tq * ct * ct, 2 * ct * ct)(
                own, gated, w_out_all[l]
            )


def solution(mesh):
    inner = Mesh(mesh.devices.reshape(NQ, NK, NC), ("q", "k", "col"))
    rows = ("q", "k")
    placed = (
        P(rows, None),
        P(),
        P(None, None, "col"),
        P(None, rows, None),
        P(None, "col"),
        P(rows),
        P(rows, None),
        P(),
        P(),
        P(None, None, None, "col"),
        P(None, "col", None),
        P(rows, "col", None),
        P(),
    )
    return jax.shard_map(
        on_device, mesh=inner, in_specs=placed, out_specs=P(rows, None), check_vma=False
    )
```

time: 986 us -> 247 us (0.25)
  blocking collectives: 517 us -> 14.6 us
  waiting for transfers between devices: 267 us -> 82.2 us
  matrix products: 48.8 us -> 0 us
  Pallas kernels: 0 us -> 35.1 us
  local copies, waits for them, and re-layouts: 52.9 us -> 35.3 us
    all_gather x4 -> x1, blocking collectives: 359 us -> 14.6 us  [on_device(): singles = lax.all_gather(token_single, 'k', axis=0, tiled=True)]
    unnamed x1 -> x0, blocking collectives: 158 us -> none
    unnamed x5 -> x2, waiting for transfers between devices: 141 us -> 0.71 us
    psum x3 -> x0, waiting for transfers between devices: 127 us -> none  [the longest x2 81.1 us: on_device(): lax.psum(partial_out.astype(jnp.bfloat16), 'col').astype(jnp.float32)]
    all_to_all x2 -> x9, waiting for transfers between devices: 0.08 us -> 67.4 us  [the longest x2 33.4 us: on_device(): lax.all_to_all(local_bias[l], ('k', 'col'), 0, 0, tiled=True)]
    dot_general x18 -> x0, matrix products: 48.8 us -> none  [the longest x2 16.5 us: on_device(): jnp.einsum('ijc,ch->hij', pair, w_bias[layer_idx], preferred_element_type...]
    pallas_call x0 -> x7, Pallas kernels: none -> 35.1 us  [the longest x2 10.8 us: on_device(): call(attend_kernel, shaped((NK, hd, tq), BF), 4 * span * NQ * span * hd,...]
    convert_element_type x8 -> x0, local copies, waits for them, and re-layouts: 22.4 us -> none  [the longest x4 19.1 us: on_device(): pair_bias.astype(jnp.float32)]
  transfers between devices with their start and end apart: 8 -> 13, of which waited for: 5 -> 8; matrix products, arithmetic and copies ran while one was open for 7% -> 11% of each run, Pallas kernels for 0% -> 6%
where the time goes in v1:
time: 247 us; the launch traced here: 246 us
  waiting for transfers between devices  82.2 us (33%)
  starting transfers between devices  60.9 us (25%)
  local copies, waits for them, and re-layouts  35.3 us (14%)
  Pallas kernels  35.1 us (14%)
  blocking collectives  14.6 us (6%)
  between operations  13.6 us (6%)
  other arithmetic  3.88 us (2%)
    all_to_all x2, waiting for transfers between devices, on_device(): lax.all_to_all(local_bias[l], ('k', 'col'), 0, 0, tiled=True)  33.4 us
    all_to_all x4, starting transfers between devices, spread_all(): lax.all_to_all(jnp.broadcast_to(x[None], (n,) + x.shape), axis, 0, 0, til...  24.5 us
    all_to_all x4, waiting for transfers between devices, spread_all(): lax.all_to_all(jnp.broadcast_to(x[None], (n,) + x.shape), axis, 0, 0, til...  17.3 us
    all_gather x1, blocking collectives, on_device(): singles = lax.all_gather(token_single, 'k', axis=0, tiled=True)  14.6 us
    all_gather x2, waiting for transfers between devices, on_device(): lax.all_gather(w_out[l], 'col', axis=0, tiled=False).reshape(NC, NK, hd, ct)  14 us
    all_to_all x2, starting transfers between devices, on_device(): lax.all_to_all(local_bias[l], ('k', 'col'), 0, 0, tiled=True)  12.3 us
    all_to_all x1, starting transfers between devices, on_device(): lax.all_to_all(counts, row_axes, 0, 0, tiled=True)[:, 0, :tq].reshape(-1)  11 us
    pallas_call x2, Pallas kernels, on_device(): call(attend_kernel, shaped((NK, hd, tq), BF), 4 * span * NQ * span * hd,...  10.8 us
  transfers between devices with their start and end apart: 13, of which 8 were waited for; matrix products, arithmetic and copies ran while one was open for 11% of the time, Pallas kernels for 6%

profile of v1, /device:TPU:1, one launch (start us, length us, event | category | flops | bytes accessed | tf_op | source)
XLA Modules:
  0.0 245.6 jit_solution(8478868318036575209)
XLA Ops:
  7.3 4.4 %collective-permute-start = (bf16[48,128]{1,0:T(8,128)(2,1)S(1)}, bf16[48,128]{1,0:T(8,128)(2,1)S(1)}, u32[]{:S(2)}, u32[]{:S(2)}) collective-permute-start(bf16[48,128]{1,0:T(8,128)(2,1)S(1)} %get-tuple-element.30), channel_id=1, source_target_pairs={{0,4},{4,8},{8,12},{12,16},{16,20},{20,24},{24,28},{28,32},{32,36}... | collective-permute-start | bytes 36872 | tf_op jit(solution)/shard_map/ppermute | solution.py:182
  14.3 11.0 %all-to-all-start = ((s32[32,8,128]{2,1,0:T(8,128)}), s32[32,8,128]{2,1,0:T(8,128)S(1)}, u32[]{:S(2)}, u32[]{:S(2)}) async-start(s32[32,8,128]{2,1,0:T(8,128)} %broadcast_in_dim.20), calls=%async_computation | async-start | bytes 262144 | tf_op jit(solution)/shard_map/all_to_all | solution.py:186
  29.1 5.0 %all-to-all-done = s32[32,8,128]{2,1,0:T(8,128)S(1)} async-done(((s32[32,8,128]{2,1,0:T(8,128)}), s32[32,8,128]{2,1,0:T(8,128)S(1)}, u32[]{:S(2)}, u32[]{:S(2)}) %all-to-all-start) | async-done | bytes 131104 | tf_op jit(solution)/shard_map/all_to_all | solution.py:186
  36.3 4.9 %shard_map.127 = bf16[8,32,320]{2,1,0:T(8,128)(2,1)} custom-call(s32[1]{0:T(128)} %bitcast.first_ref, f32[16]{0:T(128)} %bitcast_convert_fusion.wab_ref, bf16[640,128]{1,0:T(8,128)(2,1)} %feats_ref.1, bf16[48,128]{1,0:T(8,128)(2,1)} %copy-done.7, bf16[48,128]{1,0:T(8,128)(2,1)} %copy-done.8, f32[1,128]{1,0:T(1,128)} %bitcast.59, ...), custom_call_target="tpu_custom_call" | custom-call | flops 131072000 | bytes 2621440 | tf_op jit(solution)/shard_map/pallas_call | solution.py:207
  45.3 6.7 %all-to-all-done.1 = bf16[8,32,320]{2,1,0:T(8,128)(2,1)S(1)} async-done(((bf16[8,32,320]{2,1,0:T(8,128)(2,1)}), bf16[8,32,320]{2,1,0:T(8,128)(2,1)S(1)}, u32[]{:S(2)}, u32[]{:S(2)}) %all-to-all-start.1) | async-done | bytes 163872 | tf_op jit(solution)/shard_map/all_to_all | solution.py:219
  52.7 7.1 %all-to-all-start.2 = ((bf16[16,32,320]{2,1,0:T(8,128)(2,1)}), bf16[16,32,320]{2,1,0:T(8,128)(2,1)S(1)}, u32[]{:S(2)}, u32[]{:S(2)}) async-start(bf16[16,32,320]{2,1,0:T(8,128)(2,1)} %broadcast_in_dim.21), calls=%async_computation.2 | async-start | bytes 786432 | tf_op jit(solution)/shard_map/all_to_all | solution.py:165
  61.0 14.6 %all_gather.9.single_ref = bf16[320,768]{1,0:T(8,128)(2,1)} all-gather(bf16[80,768]{1,0:T(8,128)(2,1)S(1)} %copy-done.5), channel_id=1, replica_groups=mesh['q'=8,'k'=4,'col'=4] {'k'}, dimensions={0}, use_global_device_ids=true | all-gather | bytes 614400 | tf_op jit(solution)/shard_map/all_gather | solution.py:187
  82.0 3.5 %all-to-all-start.3 = ((bf16[8,320,96]{1,2,0:T(8,128)(2,1)}), bf16[8,320,96]{1,2,0:T(8,128)(2,1)S(1)}, u32[]{:S(2)}, u32[]{:S(2)}) async-start(bf16[8,320,96]{1,2,0:T(8,128)(2,1)} %broadcast_in_dim.23), calls=%async_computation.3 | async-start | bytes 1179648 | tf_op jit(solution)/shard_map/all_to_all | solution.py:165
  86.1 10.1 %shard_map.129 = bf16[2,16,80,640]{3,2,1,0:T(8,128)(2,1)} custom-call(bf16[80,640,128]{2,1,0:T(8,128)(2,1)} %pair_ref.1, bf16[32,128]{1,0:T(8,128)(2,1)} %bitcast.57), custom_call_target="tpu_custom_call" | custom-call | flops 419430400 | bytes 16384000 | tf_op jit(solution)/shard_map/pallas_call | solution.py:60
  96.2 3.9 %slice_bitcast_fusion = (bf16[16,80,640]{2,1,0:T(8,128)(2,1)}, bf16[16,80,640]{2,1,0:T(8,128)(2,1)}) fusion(bf16[2,16,80,640]{3,2,1,0:T(8,128)(2,1)} %shard_map.129), kind=kLoop, calls=%fused_computation | loop fusion | bytes 6553600 | tf_op jit(solution)/shard_map/squeeze | solution.py:200
  100.2 5.5 %all-to-all-start.4 = ((bf16[16,80,640]{2,1,0:T(8,128)(2,1)}), bf16[16,80,640]{2,1,0:T(8,128)(2,1)S(1)}, u32[]{:S(2)}, u32[]{:S(2)}) async-start(bf16[16,80,640]{2,1,0:T(8,128)(2,1)} %get-tuple-element.18), calls=%async_computation.4 | async-start | bytes 3276800 | tf_op jit(solution)/shard_map/all_to_all | solution.py:200
  107.8 22.9 %all-to-all-done.4.bias_ref = bf16[16,80,640]{2,1,0:T(8,128)(2,1)S(1)} async-done(((bf16[16,80,640]{2,1,0:T(8,128)(2,1)}), bf16[16,80,640]{2,1,0:T(8,128)(2,1)S(1)}, u32[]{:S(2)}, u32[]{:S(2)}) %all-to-all-start.4) | async-done | bytes 1638432 | tf_op jit(solution)/shard_map/all_to_all | solution.py:200
  131.9 5.4 %shard_map.130 = bf16[4,48,80]{2,1,0:T(8,128)(2,1)} custom-call(bf16[320,96]{1,0:T(8,128)(2,1)} %get-tuple-element.12.qg_ref, bf16[2560,96]{1,0:T(8,128)(2,1)} %bitcast.41, bf16[16,80,640]{2,1,0:T(8,128)(2,1)} %copy-done.1), custom_call_target="tpu_custom_call" | custom-call | flops 157286400 | bytes 1638400 | tf_op jit(solution)/shard_map/pallas_call | solution.py:230
  139.2 5.4 %all-to-all-start.5 = ((bf16[16,4,48,80]{3,2,1,0:T(8,128)(2,1)}), bf16[16,4,48,80]{3,2,1,0:T(8,128)(2,1)S(1)}, u32[]{:S(2)}, u32[]{:S(2)}) async-start(bf16[16,4,48,80]{3,2,1,0:T(8,128)(2,1)} %broadcast_in_dim.24), calls=%async_computation.5 | async-start | bytes 1572864 | tf_op jit(solution)/shard_map/all_to_all | solution.py:165
  148.8 8.8 %all-to-all-done.5 = bf16[16,4,48,80]{3,2,1,0:T(8,128)(2,1)S(1)} async-done(((bf16[16,4,48,80]{3,2,1,0:T(8,128)(2,1)}), bf16[16,4,48,80]{3,2,1,0:T(8,128)(2,1)S(1)}, u32[]{:S(2)}, u32[]{:S(2)}) %all-to-all-start.5) | async-done | bytes 491552 | tf_op jit(solution)/shard_map/all_to_all | solution.py:165
  158.5 3.9 %shard_map.131 = (f32[320,768]{1,0:T(8,128)}, bf16[320,96]{1,0:T(8,128)(2,1)}, bf16[320,96]{1,0:T(8,128)(2,1)}) custom-call(f32[320,768]{1,0:T(8,128)} %get-tuple-element.11.res_ref, bf16[4,768,80]{2,1,0:T(8,128)(2,1)} %bitcast.40, bf16[768,768]{1,0:T(8,128)(2,1)} %bitcast.37, f32[1,768]{1,0:T(1,128)} %get-tuple-element.33.gain_ref, ...), custom_call_target="tpu_custom_call" | custom-call | flops 471859200 | bytes 3072000 | tf_op jit(solution)/shard_map/pallas_call | solution.py:236
  164.3 8.5 %all-to-all-start.6 = ((bf16[8,320,96]{1,2,0:T(8,128)(2,1)}), bf16[8,320,96]{1,2,0:T(8,128)(2,1)S(1)}, u32[]{:S(2)}, u32[]{:S(2)}) async-start(bf16[8,320,96]{1,2,0:T(8,128)(2,1)} %broadcast_in_dim.25), calls=%async_computation.6 | async-start | bytes 1179648 | tf_op jit(solution)/shard_map/all_to_all | solution.py:165
  173.6 8.5 %all-to-all-done.6 = bf16[8,320,96]{1,2,0:T(8,128)(2,1)S(1)} async-done(((bf16[8,320,96]{1,2,0:T(8,128)(2,1)}), bf16[8,320,96]{1,2,0:T(8,128)(2,1)S(1)}, u32[]{:S(2)}, u32[]{:S(2)}) %all-to-all-start.6) | async-done | bytes 491552 | tf_op jit(solution)/shard_map/all_to_all | solution.py:165
  182.1 6.9 %all-to-all-start.7 = ((bf16[16,80,640]{2,1,0:T(8,128)(2,1)}), bf16[16,80,640]{2,1,0:T(8,128)(2,1)S(1)}, u32[]{:S(2)}, u32[]{:S(2)}) async-start(bf16[16,80,640]{2,1,0:T(8,128)(2,1)} %get-tuple-element.17), calls=%async_computation.7 | async-start | bytes 3276800 | tf_op jit(solution)/shard_map/all_to_all | solution.py:200
  189.0 14.0 %all-gather.5.cloned.1.call-done = bf16[4,192,768]{2,1,0:T(8,128)(2,1)} async-done(((bf16[1,192,768]{2,1,0:T(8,128)(2,1)}), bf16[4,192,768]{2,1,0:T(8,128)(2,1)}) %all-gather.5.cloned.1.call-update) | async-done | bytes 1179664 | tf_op jit(solution)/shard_map/all_gather | solution.py:189
  206.5 10.4 %all-to-all-done.7.bias_ref = bf16[16,80,640]{2,1,0:T(8,128)(2,1)S(1)} async-done(((bf16[16,80,640]{2,1,0:T(8,128)(2,1)}), bf16[16,80,640]{2,1,0:T(8,128)(2,1)S(1)}, u32[]{:S(2)}, u32[]{:S(2)}) %all-to-all-start.7) | async-done | bytes 1638432 | tf_op jit(solution)/shard_map/all_to_all | solution.py:200
  218.1 5.4 %shard_map.132 = bf16[4,48,80]{2,1,0:T(8,128)(2,1)} custom-call(bf16[320,96]{1,0:T(8,128)(2,1)} %get-tuple-element.15.qg_ref, bf16[2560,96]{1,0:T(8,128)(2,1)} %bitcast.42, bf16[16,80,640]{2,1,0:T(8,128)(2,1)} %copy-done), custom_call_target="tpu_custom_call" | custom-call | flops 157286400 | bytes 1638400 | tf_op jit(solution)/shard_map/pallas_call | solution.py:230
  225.0 3.9 %all-to-all-start.8 = ((bf16[16,48,80]{2,1,0:T(8,128)(2,1)}), bf16[16,48,80]{2,1,0:T(8,128)(2,1)S(1)}, u32[]{:S(2)}, u32[]{:S(2)}) async-start(bf16[16,48,80]{2,1,0:T(8,128)(2,1)} %bitcast.24), calls=%async_computation.8 | async-start | bytes 393216 | tf_op jit(solution)/shard_map/all_to_all | solution.py:241
  230.6 5.1 %all-to-all-done.8 = bf16[16,48,80]{2,1,0:T(8,128)(2,1)S(1)} async-done(((bf16[16,48,80]{2,1,0:T(8,128)(2,1)}), bf16[16,48,80]{2,1,0:T(8,128)(2,1)S(1)}, u32[]{:S(2)}, u32[]{:S(2)}) %all-to-all-start.8) | async-done | bytes 122912 | tf_op jit(solution)/shard_map/all_to_all | solution.py:241
  (83 shorter events, 46.3 us)
Async XLA Ops:
  6.5 22.1 %copy-start.11 = (bf16[16,1]{0,1:T(2,128)(2,1)S(1)}, bf16[16,1]{0,1:T(2,128)(2,1)}, u32[]{:S(2)}) copy-start(bf16[16,1]{0,1:T(2,128)(2,1)} %param.17) | copy-start | bytes 100
  7.3 28.4 %collective-permute-start = (bf16[48,128]{1,0:T(8,128)(2,1)S(1)}, bf16[48,128]{1,0:T(8,128)(2,1)S(1)}, u32[]{:S(2)}, u32[]{:S(2)}) collective-permute-start(bf16[48,128]{1,0:T(8,128)(2,1)S(1)} %get-tuple-element.30), channel_id=1, source_target_pairs={{0,4},{4,8},{8,12},{12,16},{16,20},{20,24},{24,28},{28,32},{32,36}... | collective-permute-start | bytes 36872 | tf_op jit(solution)/shard_map/ppermute | solution.py:182
  11.6 24.0 %collective-permute-start.1 = (bf16[48,128]{1,0:T(8,128)(2,1)S(1)}, bf16[48,128]{1,0:T(8,128)(2,1)S(1)}, u32[]{:S(2)}, u32[]{:S(2)}) collective-permute-start(bf16[48,128]{1,0:T(8,128)(2,1)S(1)} %get-tuple-element.29), channel_id=1, source_target_pairs={{4,0},{8,4},{12,8},{16,12},{20,16},{24,20},{28,24},{32,28},{36,32}... | collective-permute-start | bytes 36872 | tf_op jit(solution)/shard_map/ppermute | solution.py:183
  14.3 19.9 %all-to-all-start = ((s32[32,8,128]{2,1,0:T(8,128)}), s32[32,8,128]{2,1,0:T(8,128)S(1)}, u32[]{:S(2)}, u32[]{:S(2)}) async-start(s32[32,8,128]{2,1,0:T(8,128)} %broadcast_in_dim.20), calls=%async_computation | async-start | bytes 262144 | tf_op jit(solution)/shard_map/all_to_all | solution.py:186
  34.9 0.7 copy-start.6
  35.6 0.6 copy-start.7
  36.3 8.4 %copy-start.10 = (f32[2,768]{1,0:T(2,128)S(1)}, f32[2,768]{1,0:T(2,128)}, u32[]{:S(2)}) copy-start(f32[2,768]{1,0:T(2,128)} %param.21) | copy-start | bytes 18436
  41.1 19.9 %copy-start.5 = (bf16[80,768]{1,0:T(8,128)(2,1)S(1)}, bf16[80,768]{1,0:T(8,128)(2,1)}, u32[]{:S(2)}) copy-start(bf16[80,768]{1,0:T(8,128)(2,1)} %param.19) | copy-start | bytes 368644
  41.1 10.8 %all-to-all-start.1 = ((bf16[8,32,320]{2,1,0:T(8,128)(2,1)}), bf16[8,32,320]{2,1,0:T(8,128)(2,1)S(1)}, u32[]{:S(2)}, u32[]{:S(2)}) async-start(bf16[8,32,320]{2,1,0:T(8,128)(2,1)} %shard_map.127), calls=%async_computation.1 | async-start | bytes 393216 | tf_op jit(solution)/shard_map/all_to_all | solution.py:219
  52.7 23.6 %all-to-all-start.2 = ((bf16[16,32,320]{2,1,0:T(8,128)(2,1)}), bf16[16,32,320]{2,1,0:T(8,128)(2,1)S(1)}, u32[]{:S(2)}, u32[]{:S(2)}) async-start(bf16[16,32,320]{2,1,0:T(8,128)(2,1)} %broadcast_in_dim.21), calls=%async_computation.2 | async-start | bytes 786432 | tf_op jit(solution)/shard_map/all_to_all | solution.py:165
  76.4 0.8 copy-start.2
  77.1 8.4 %copy-start.9 = (bf16[2,128,16]{1,2,0:T(8,128)(2,1)S(1)}, bf16[2,128,16]{1,2,0:T(8,128)(2,1)}, u32[]{:S(2)}) copy-start(bf16[2,128,16]{1,2,0:T(8,128)(2,1)} %param.25) | copy-start | bytes 24580
  82.0 18.2 %all-to-all-start.3 = ((bf16[8,320,96]{1,2,0:T(8,128)(2,1)}), bf16[8,320,96]{1,2,0:T(8,128)(2,1)S(1)}, u32[]{:S(2)}, u32[]{:S(2)}) async-start(bf16[8,320,96]{1,2,0:T(8,128)(2,1)} %broadcast_in_dim.23), calls=%async_computation.3 | async-start | bytes 1179648 | tf_op jit(solution)/shard_map/all_to_all | solution.py:165
  100.2 5.5 %copy-start.4 = (bf16[2,192,768]{2,1,0:T(8,128)(2,1)S(1)}, bf16[2,192,768]{2,1,0:T(8,128)(2,1)}, u32[]{:S(2)}) copy-start(bf16[2,192,768]{2,1,0:T(8,128)(2,1)} %param.23) | copy-start | bytes 1769476
  100.2 30.6 %all-to-all-start.4 = ((bf16[16,80,640]{2,1,0:T(8,128)(2,1)}), bf16[16,80,640]{2,1,0:T(8,128)(2,1)S(1)}, u32[]{:S(2)}, u32[]{:S(2)}) async-start(bf16[16,80,640]{2,1,0:T(8,128)(2,1)} %get-tuple-element.18), calls=%async_computation.4 | async-start | bytes 3276800 | tf_op jit(solution)/shard_map/all_to_all | solution.py:200
  105.6 40.8 %all-gather.3.cloned.1.call-start = ((), (), s32[]{:S(2)}) async-start(), calls=%async_computation.9 | async-start | bytes 1474560 | tf_op jit(solution)/shard_map/all_gather | solution.py:189
  130.7 1.2 copy-start.1
  139.2 18.3 %all-to-all-start.5 = ((bf16[16,4,48,80]{3,2,1,0:T(8,128)(2,1)}), bf16[16,4,48,80]{3,2,1,0:T(8,128)(2,1)S(1)}, u32[]{:S(2)}, u32[]{:S(2)}) async-start(bf16[16,4,48,80]{3,2,1,0:T(8,128)(2,1)} %broadcast_in_dim.24), calls=%async_computation.5 | async-start | bytes 1572864 | tf_op jit(solution)/shard_map/all_to_all | solution.py:165
  164.3 17.8 %all-to-all-start.6 = ((bf16[8,320,96]{1,2,0:T(8,128)(2,1)}), bf16[8,320,96]{1,2,0:T(8,128)(2,1)S(1)}, u32[]{:S(2)}, u32[]{:S(2)}) async-start(bf16[8,320,96]{1,2,0:T(8,128)(2,1)} %broadcast_in_dim.25), calls=%async_computation.6 | async-start | bytes 1179648 | tf_op jit(solution)/shard_map/all_to_all | solution.py:165
  172.8 30.2 %all-gather.5.cloned.1.call-start = ((), (), s32[]{:S(2)}) async-start(), calls=%async_computation.10 | async-start | bytes 1474560 | tf_op jit(solution)/shard_map/all_gather | solution.py:189
  182.1 34.8 %all-to-all-start.7 = ((bf16[16,80,640]{2,1,0:T(8,128)(2,1)}), bf16[16,80,640]{2,1,0:T(8,128)(2,1)S(1)}, u32[]{:S(2)}, u32[]{:S(2)}) async-start(bf16[16,80,640]{2,1,0:T(8,128)(2,1)} %get-tuple-element.17), calls=%async_computation.7 | async-start | bytes 3276800 | tf_op jit(solution)/shard_map/all_to_all | solution.py:200
  216.9 1.2 copy-start
  225.0 10.6 %all-to-all-start.8 = ((bf16[16,48,80]{2,1,0:T(8,128)(2,1)}), bf16[16,48,80]{2,1,0:T(8,128)(2,1)S(1)}, u32[]{:S(2)}, u32[]{:S(2)}) async-start(bf16[16,48,80]{2,1,0:T(8,128)(2,1)} %bitcast.24), calls=%async_computation.8 | async-start | bytes 393216 | tf_op jit(solution)/shard_map/all_to_all | solution.py:241
  235.6 0.7 copy-start.3
  (1 other events, 0.6 us)
Sparse Core Ops, SparseCore 0:
  108.1 28.7 all-gather.2
  175.3 27.6 all-gather.4
